TPU v7x, 512 devices: a whole 4x8x8 slice. The times are simulated.
512 devices in a mesh: seq: 32 (over y_hi, x, core), dp: 16 (over z, y_lo).
Axes of the slice: x: 4, y: 8 (y_hi: 4, y_lo: 2; y = y_hi * 2 + y_lo), z: 8, core: 2. Of those that a mesh axis runs over, the one named last changes fastest.
Arguments:
- span_queries: bfloat16 [4096, 4096], P('seq', 'dp'), may hold values from -2.5 to 2.5
- output_grad: bfloat16 [4096, 4096], P('seq', 'dp'), may hold values from -6 to 6
- neighbour_keys: bfloat16 [16384, 4096], P('seq', 'dp'), may hold values from -2.5 to 2.5
- neighbour_states: bfloat16 [16384, 4096], P('seq', 'dp'), may hold values from -6 to 6
- encoder_queries: bfloat16 [16384, 4096], P('seq', 'dp'), may hold values from -2.5 to 2.5
- span_keys: bfloat16 [4096, 4096], P('seq', 'dp'), may hold values from -2.5 to 2.5
- span_values: bfloat16 [4096, 4096], P('seq', 'dp'), may hold values from -6 to 6
- norm_gain: float32 [4096], P('dp'), may hold values from 0.25 to 1.75
Outputs:
- query_grad: bfloat16 [4096, 4096], P('seq', 'dp')
- key_grad: bfloat16 [16384, 4096], P('seq', 'dp')
- state_grad: bfloat16 [16384, 4096], P('seq', 'dp')
- encoder_query_grad: bfloat16 [16384, 4096], P('seq', 'dp')
- span_key_grad: bfloat16 [4096, 4096], P('seq', 'dp')
- span_value_grad: bfloat16 [4096, 4096], P('seq', 'dp')
- gain_grad: float32 [4096], P('dp')
All inputs are finite; a program needn't handle non-finite values.
Results may differ from a plain program's by a relative error of at most 0.0064.
Values may be sent and summed in bfloat16 or wider, within the bound.
A program may use at most 64 MiB of HBM per device.

v0:
```python
import jax
import jax.numpy as jnp
from jax import lax
from jax.sharding import PartitionSpec as P

HD = 128
SPAN = 64
MEM = 256
WIDTH = 4096


norm_eps = 1e-05


def passed_along(shard, axis, by):
    size = lax.axis_size(axis)
    pairs = [(i, i + by) for i in range(size) if 0 <= i + by < size]
    return lax.ppermute(shard, axis, pairs)


def attend_spans(queries, grads, keys, values, head_count):
    groups = queries.shape[0] // SPAN
    width = queries.shape[1]
    score_scale = HD ** (-0.5)
    query_blocks = queries.reshape(groups, SPAN, head_count, HD)
    grad_blocks = grads.reshape(groups, SPAN, head_count, HD)
    key_blocks = keys.reshape(groups, MEM, head_count, HD)
    value_blocks = values.reshape(groups, MEM, head_count, HD)
    scores = (
        jnp.einsum("cqhd,cmhd->chqm", query_blocks, key_blocks, preferred_element_type=jnp.float32)
        * score_scale
    )
    weights = jnp.exp(scores)
    weights = weights / jnp.sum(weights, axis=-1, keepdims=True)
    weights_low = weights.astype(jnp.bfloat16)
    d_weights = jnp.einsum(
        "cqhd,cmhd->chqm", grad_blocks, value_blocks, preferred_element_type=jnp.float32
    )
    delta_sum = jnp.sum(weights * d_weights, axis=-1, keepdims=True)
    d_scores = (weights * (d_weights - delta_sum) * score_scale).astype(jnp.bfloat16)
    d_query = jnp.einsum(
        "chqm,cmhd->cqhd", d_scores, key_blocks, preferred_element_type=jnp.float32
    ).reshape(groups * SPAN, width)
    d_key = jnp.einsum(
        "chqm,cqhd->cmhd", d_scores, query_blocks, preferred_element_type=jnp.float32
    ).reshape(groups * MEM, width)
    d_value = jnp.einsum(
        "chqm,cqhd->cmhd", weights_low, grad_blocks, preferred_element_type=jnp.float32
    ).reshape(groups * MEM, width)
    return (d_query, d_key, d_value)


def shards(
    span_queries,
    output_grad,
    neighbour_keys,
    neighbour_states,
    encoder_queries,
    span_keys,
    span_values,
    norm_gain,
):
    row_count, width = span_queries.shape
    head_count = width // HD
    groups = row_count // SPAN
    score_scale = HD ** (-0.5)
    enc_q = encoder_queries.reshape(groups, MEM, head_count, HD)
    enc_k = span_keys.reshape(groups, SPAN, head_count, HD)
    enc_v = span_values.reshape(groups, SPAN, head_count, HD)
    enc_scores = (
        jnp.einsum("cmhd,cthd->chmt", enc_q, enc_k, preferred_element_type=jnp.float32)
        * score_scale
    )
    enc_weights = jnp.exp(enc_scores)
    enc_weights = enc_weights / jnp.sum(enc_weights, axis=-1, keepdims=True)
    enc_low = enc_weights.astype(jnp.bfloat16)
    attended = jnp.einsum("chmt,cthd->cmhd", enc_low, enc_v, preferred_element_type=jnp.float32)
    encoded = (
        neighbour_states.astype(jnp.float32).reshape(groups, MEM, head_count, HD) + attended
    ).reshape(groups * MEM, width)
    totals = lax.psum(jnp.sum(encoded * encoded, axis=-1), "dp")
    inverse = lax.rsqrt(totals[:, None] / WIDTH + norm_eps)
    normed = (encoded * inverse * norm_gain).astype(jnp.bfloat16)
    prior_keys, prior_values = passed_along((neighbour_keys[-MEM:], normed[-MEM:]), "seq", 1)
    key_rows = jnp.concatenate([prior_keys, neighbour_keys], axis=0)
    value_rows = jnp.concatenate([prior_values, normed], axis=0)
    pad_front = jnp.zeros((1, width), jnp.bfloat16)
    pad_back = jnp.zeros((SPAN - 1, width), jnp.bfloat16)
    query_rows = jnp.concatenate([pad_front, span_queries, pad_back], axis=0)
    grad_rows = jnp.concatenate([pad_front, output_grad, pad_back], axis=0)
    d_query, d_key, d_value = attend_spans(query_rows, grad_rows, key_rows, value_rows, head_count)
    back_key, back_value = passed_along((d_key[:MEM], d_value[:MEM]), "seq", -1)
    lead_zeros = jnp.zeros(((groups - 1) * MEM, width), jnp.float32)
    d_key = d_key[MEM:] + jnp.concatenate([lead_zeros, back_key], axis=0)
    d_value = d_value[MEM:] + jnp.concatenate([lead_zeros, back_value], axis=0)
    query_grad = d_query[1 : row_count + 1].astype(jnp.bfloat16)
    key_grad = d_key.astype(jnp.bfloat16)
    gain_grad = lax.psum(jnp.sum(d_value * encoded * inverse, axis=0), "seq")
    scaled_grad = d_value * norm_gain
    grad_dot = lax.psum(jnp.sum(scaled_grad * encoded, axis=-1), "dp")
    state_grad = (
        inverse * (scaled_grad - encoded * grad_dot[:, None] * inverse * inverse / WIDTH)
    ).astype(jnp.bfloat16)
    back_rows = state_grad.reshape(groups, MEM, head_count, HD)
    d_enc_weights = jnp.einsum(
        "cmhd,cthd->chmt", back_rows, enc_v, preferred_element_type=jnp.float32
    )
    enc_delta = jnp.sum(enc_weights * d_enc_weights, axis=-1, keepdims=True)
    d_enc_scores = (enc_weights * (d_enc_weights - enc_delta) * score_scale).astype(jnp.bfloat16)
    encoder_query_grad = (
        jnp.einsum("chmt,cthd->cmhd", d_enc_scores, enc_k, preferred_element_type=jnp.float32)
        .reshape(groups * MEM, width)
        .astype(jnp.bfloat16)
    )
    span_key_grad = (
        jnp.einsum("chmt,cmhd->cthd", d_enc_scores, enc_q, preferred_element_type=jnp.float32)
        .reshape(row_count, width)
        .astype(jnp.bfloat16)
    )
    span_value_grad = (
        jnp.einsum("chmt,cmhd->cthd", enc_low, back_rows, preferred_element_type=jnp.float32)
        .reshape(row_count, width)
        .astype(jnp.bfloat16)
    )
    return (
        query_grad,
        key_grad,
        state_grad,
        encoder_query_grad,
        span_key_grad,
        span_value_grad,
        gain_grad,
    )


def solution(mesh):
    return jax.shard_map(
        shards,
        mesh=mesh,
        in_specs=(
            P("seq", "dp"),
            P("seq", "dp"),
            P("seq", "dp"),
            P("seq", "dp"),
            P("seq", "dp"),
            P("seq", "dp"),
            P("seq", "dp"),
            P("dp"),
        ),
        out_specs=(
            P("seq", "dp"),
            P("seq", "dp"),
            P("seq", "dp"),
            P("seq", "dp"),
            P("seq", "dp"),
            P("seq", "dp"),
            P("dp"),
        ),
        check_vma=False,
    )
```

profile of v0, /device:TPU:32, one launch (start us, length us, event | category | flops | bytes accessed | tf_op | source)
XLA Modules:
  0.0 183.8 jit_solution(5626195451806773660)
XLA Ops:
  0.7 1.0 slice.34
  1.6 1.9 %collective-permute-start = (bf16[256,256]{1,0:T(8,128)(2,1)S(1)}, bf16[256,256]{1,0:T(8,128)(2,1)S(1)}, u32[]{:S(2)}, u32[]{:S(2)}) collective-permute-start(bf16[256,256]{1,0:T(8,128)(2,1)S(1)} %slice.34), channel_id=1, source_target_pairs={{0,16},{16,32},{32,48},{48,64},{64,80},{80,96},{96,112},{112,128},... | collective-permute-start | bytes 393224 | tf_op jit(solution)/shard_map/ppermute | solution.py:18
  3.5 0.1 pad.11.clone
  3.6 0.0 copy-start.5
  3.6 0.1 maximum_maximum_fusion.1
  3.8 0.8 copy-done.5
  4.6 0.3 reshape.87
  4.8 0.0 copy-start.12
  4.9 0.0 copy-start.8
  4.9 0.2 copy.30
  5.1 0.6 copy-done.12
  5.7 0.1 copy-done.8
  5.8 0.1 reshape.79
  5.9 0.8 copy-done.13
  6.7 0.2 fusion.11
  7.0 0.3 multiply_reduce_fusion.1
  7.3 39.9 %psum.21 = f32[512]{0:T(512)S(1)} all-reduce(f32[512]{0:T(512)S(1)} %bitcast.102), channel_id=1, replica_groups=mesh['seq'=32,'dp'=16] {'dp'}, use_global_device_ids=true, to_apply=%region_3.0 | all-reduce | flops 512 | bytes 4096 | tf_op jit(solution)/shard_map/psum | solution.py:81
  47.3 0.0 copy-start.2
  47.3 0.7 fusion.52
  48.0 0.0 collective-permute-done
  48.0 0.2 copy-done.2
  48.3 0.1 reshape.74
  48.4 0.3 fusion.4
  48.6 0.4 convolution_bitcast_fusion
  49.1 0.3 copy-done.3
  49.4 0.8 copy.41
  50.2 1.9 %collective-permute-start.3 = (f32[256,256]{1,0:T(8,128)}, f32[256,256]{1,0:T(8,128)S(1)}, u32[]{:S(2)}, u32[]{:S(2)}) collective-permute-start(f32[256,256]{1,0:T(8,128)} %copy.41), channel_id=1, source_target_pairs={{16,0},{32,16},{48,32},{64,48},{80,64},{96,80},{112,96},{128,112},... | collective-permute-start | bytes 786440 | tf_op jit(solution)/shard_map/ppermute | solution.py:18
  52.2 0.2 copy.31
  52.5 0.2 copy.40
  52.7 0.7 copy-done.4
  53.4 0.6 fusion.48
  54.1 3.7 %collective-permute-done.3 = f32[256,256]{1,0:T(8,128)S(1)} collective-permute-done((f32[256,256]{1,0:T(8,128)}, f32[256,256]{1,0:T(8,128)S(1)}, u32[]{:S(2)}, u32[]{:S(2)}) %collective-permute-start.3) | collective-permute-done | bytes 262176 | tf_op jit(solution)/shard_map/ppermute | solution.py:18
  57.8 0.7 copy-done.14
  58.5 0.3 fusion.32
  58.7 30.8 %psum.22 = f32[512]{0:T(512)S(1)} all-reduce(f32[512]{0:T(512)S(1)} %get-tuple-element.8), channel_id=1, replica_groups=mesh['seq'=32,'dp'=16] {'dp'}, use_global_device_ids=true, to_apply=%region_6.0 | all-reduce | flops 512 | bytes 4096 | tf_op jit(solution)/shard_map/psum | solution.py:100
  89.5 0.2 fusion.30
  89.8 0.0 copy-start.1
  89.8 0.0 copy-start.7
  89.8 0.1 reshape.85
  89.9 0.6 copy-done.1
  90.5 0.2 copy-done.7
  90.7 0.2 fusion.42
  90.9 1.2 fusion.16
  92.2 1.9 %collective-permute-start.1 = (bf16[256,256]{1,0:T(8,128)(2,1)S(1)}, bf16[256,256]{1,0:T(8,128)(2,1)S(1)}, u32[]{:S(2)}, u32[]{:S(2)}) collective-permute-start(bf16[256,256]{1,0:T(8,128)(2,1)S(1)} %slice.45), channel_id=1, source_target_pairs={{0,16},{16,32},{32,48},{48,64},{64,80},{80,96},{96,112},{112,128},... | collective-permute-start | bytes 393224 | tf_op jit(solution)/shard_map/ppermute | solution.py:18
  94.1 0.1 copy.49
  94.2 1.2 fusion.15
  95.4 0.1 copy.47
  95.5 1.3 fusion.12
  96.8 7.3 %collective-permute-done.1 = bf16[256,256]{1,0:T(8,128)(2,1)S(1)} collective-permute-done((bf16[256,256]{1,0:T(8,128)(2,1)S(1)}, bf16[256,256]{1,0:T(8,128)(2,1)S(1)}, u32[]{:S(2)}, u32[]{:S(2)}) %collective-permute-start.1) | collective-permute-done | bytes 131104 | tf_op jit(solution)/shard_map/ppermute | solution.py:18
  104.1 0.1 reshape.83
  104.2 0.2 fusion.37
  104.5 0.4 convolution_bitcast_fusion.1
  104.9 0.1 copy.38
  105.0 1.9 %collective-permute-start.2 = (f32[256,256]{1,0:T(8,128)S(1)}, f32[256,256]{1,0:T(8,128)S(1)}, u32[]{:S(2)}, u32[]{:S(2)}) collective-permute-start(f32[256,256]{1,0:T(8,128)S(1)} %copy.38), channel_id=1, source_target_pairs={{16,0},{32,16},{48,32},{64,48},{80,64},{96,80},{112,96},{128,112},... | collective-permute-start | bytes 786440 | tf_op jit(solution)/shard_map/ppermute | solution.py:18
  107.0 0.7 copy_bitcast_fusion.2
  107.6 0.3 copy.45
  107.9 0.7 copy.106
  108.7 73.1 %psum.23 = f32[256]{0:T(256)} all-reduce(f32[256]{0:T(256)S(1)} %get-tuple-element.7), channel_id=1, replica_groups=mesh['seq'=32,'dp'=16] {'seq'}, use_global_device_ids=true, to_apply=%region_9.0 | all-reduce | flops 256 | bytes 2048 | tf_op jit(solution)/shard_map/psum | solution.py:98
  181.7 0.3 fusion.14
  182.0 0.1 copy.35
  182.1 0.6 slice.46
  182.8 0.2 copy.37
  183.0 0.0 collective-permute-done.2
  183.0 0.7 fusion.21
  (31 shorter events, 0.3 us)
Async XLA Ops:
  0.6 3.0 %copy-start.10 = (bf16[128,256]{1,0:T(8,128)(2,1)S(1)}, bf16[128,256]{1,0:T(8,128)(2,1)}, u32[]{:S(2)}) copy-start(bf16[128,256]{1,0:T(8,128)(2,1)} %param.9) | copy-start | bytes 196612
  0.6 3.0 %copy-start.11 = (bf16[128,256]{1,0:T(8,128)(2,1)S(1)}, bf16[128,256]{1,0:T(8,128)(2,1)}, u32[]{:S(2)}) copy-start(bf16[128,256]{1,0:T(8,128)(2,1)} %param.8) | copy-start | bytes 196612
  1.6 46.4 %collective-permute-start = (bf16[256,256]{1,0:T(8,128)(2,1)S(1)}, bf16[256,256]{1,0:T(8,128)(2,1)S(1)}, u32[]{:S(2)}, u32[]{:S(2)}) collective-permute-start(bf16[256,256]{1,0:T(8,128)(2,1)S(1)} %slice.34), channel_id=1, source_target_pairs={{0,16},{16,32},{32,48},{48,64},{64,80},{80,96},{96,112},{112,128},... | collective-permute-start | bytes 393224 | tf_op jit(solution)/shard_map/ppermute | solution.py:18
  3.6 1.0 copy-start.5
  4.8 0.8 copy-start.12
  4.9 1.0 copy-start.8
  5.8 1.1 copy-start.6
  5.8 0.9 copy-start.13
  7.0 40.3 %copy-start.9 = (f32[2,2,256,64]{2,3,1,0:T(8,128)}, f32[2,2,256,64]{2,3,1,0:T(8,128)S(1)}, u32[]{:S(2)}) copy-start(f32[2,2,256,64]{2,3,1,0:T(8,128)S(1)} %fusion.11) | copy-start | bytes 786436
  47.3 1.0 copy-start.2
  48.6 0.7 copy-start.3
  50.2 7.5 %collective-permute-start.3 = (f32[256,256]{1,0:T(8,128)}, f32[256,256]{1,0:T(8,128)S(1)}, u32[]{:S(2)}, u32[]{:S(2)}) collective-permute-start(f32[256,256]{1,0:T(8,128)} %copy.41), channel_id=1, source_target_pairs={{16,0},{32,16},{48,32},{64,48},{80,64},{96,80},{112,96},{128,112},... | collective-permute-start | bytes 786440 | tf_op jit(solution)/shard_map/ppermute | solution.py:18
  52.4 1.0 copy-start.4
  57.8 0.7 copy-start.14
  89.8 0.7 copy-start.1
  89.8 0.9 copy-start.7
  92.2 11.9 %collective-permute-start.1 = (bf16[256,256]{1,0:T(8,128)(2,1)S(1)}, bf16[256,256]{1,0:T(8,128)(2,1)S(1)}, u32[]{:S(2)}, u32[]{:S(2)}) collective-permute-start(bf16[256,256]{1,0:T(8,128)(2,1)S(1)} %slice.45), channel_id=1, source_target_pairs={{0,16},{16,32},{32,48},{48,64},{64,80},{80,96},{96,112},{112,128},... | collective-permute-start | bytes 393224 | tf_op jit(solution)/shard_map/ppermute | solution.py:18
  104.9 76.8 %copy-start = (f32[3,256,2,128]{1,3,2,0:T(8,128)}, f32[3,256,2,128]{1,3,2,0:T(8,128)S(1)}, u32[]{:S(2)}) copy-start(f32[3,256,2,128]{1,3,2,0:T(8,128)S(1)} %convolution_bitcast_fusion.1) | copy-start | bytes 2359300
  105.0 78.0 %collective-permute-start.2 = (f32[256,256]{1,0:T(8,128)S(1)}, f32[256,256]{1,0:T(8,128)S(1)}, u32[]{:S(2)}, u32[]{:S(2)}) collective-permute-start(f32[256,256]{1,0:T(8,128)S(1)} %copy.38), channel_id=1, source_target_pairs={{16,0},{32,16},{48,32},{64,48},{80,64},{96,80},{112,96},{128,112},... | collective-permute-start | bytes 786440 | tf_op jit(solution)/shard_map/ppermute | solution.py:18
  181.7 1.1 slice-start
where the time goes:
time: 184 us
  blocking collectives  144 us (78%)
  local copies, waits for them, and re-layouts  11.4 us (6%)
  waiting for transfers between devices  11 us (6%)
  starting transfers between devices  7.67 us (4%)
  matrix products  6.1 us (3%)
  other arithmetic  2.77 us (2%)
    psum x1, blocking collectives, shards(): gain_grad = lax.psum(jnp.sum(d_value * encoded * inverse, axis=0), 'seq')  73.1 us
    psum x1, blocking collectives, shards(): totals = lax.psum(jnp.sum(encoded * encoded, axis=-1), 'dp')  39.9 us
    psum x1, blocking collectives, shards(): grad_dot = lax.psum(jnp.sum(scaled_grad * encoded, axis=-1), 'dp')  30.8 us
    ppermute x4, waiting for transfers between devices, passed_along(): return lax.ppermute(shard, axis, pairs)  11 us
    ppermute x4, starting transfers between devices, passed_along(): return lax.ppermute(shard, axis, pairs)  7.67 us
    unnamed x33, local copies, waits for them, and re-layouts  5.92 us
  transfers between devices with their start and end apart: 4, of which 2 were waited for; matrix products, arithmetic and copies ran while one was open for 5% of the time, Pallas kernels for 0%

commit v1 on v0

v1 whole, which is shorter than its diff:
```python
import functools

import jax
import jax.numpy as jnp
from jax import lax
from jax.experimental import pallas as pl
from jax.experimental.pallas import tpu as pltpu
from jax.sharding import PartitionSpec as P

HD = 128
SPAN = 64
MEM = 256
NORM_EPS = 1e-05
SCALE = HD ** (-0.5)
MESH = pl.DeviceIdType.MESH
F32 = jnp.float32
BF16 = jnp.bfloat16


def nt(a, b):
    return lax.dot_general(a, b, (((1,), (1,)), ((), ())), preferred_element_type=F32)


def nn(a, b):
    return lax.dot_general(a, b, (((1,), (0,)), ((), ())), preferred_element_type=F32)


def tn(a, b):
    return lax.dot_general(a, b, (((0,), (0,)), ((), ())), preferred_element_type=F32)


def two_heads(x):
    first = lax.broadcasted_iota(jnp.int32, x.shape, 1) < HD
    zero = jnp.zeros_like(x)
    return jnp.concatenate([jnp.where(first, x, zero), jnp.where(first, zero, x)], axis=0)


def diagonal(x):
    first = lax.broadcasted_iota(jnp.int32, (SPAN, 2 * HD), 1) < HD
    return jnp.where(first, x[:SPAN], x[SPAN:])


def half_sums(x, left):
    zero = jnp.zeros_like(x)
    first = jnp.sum(jnp.where(left, x, zero), axis=1, keepdims=True)
    last = jnp.sum(jnp.where(left, zero, x), axis=1, keepdims=True)
    return first, last


def kernel(
    n_seq, n_dp, inner, sq_h, og_h, nk_h, ns_h, eq_h, sk_h, sv_h, gain_h,
    qg_h, kg_h, sg_h, eqg_h, skg_h, svg_h, gg_h,
    sq, og, nk, ns, eq, sk, sv, gain,
    qg, kg, sg, eqg, skg, svg, gg,
    next_q, next_g, dq_out, dq_in, enc, enc_w, enc_low, val, weights,
    part_out, part_in, gain_out, gain_in, gain_out2, gain_in2,
    in_sem, out_sem, halo_send, halo_recv, back_send, back_recv,
    part_send, part_recv, gain_send, gain_recv, gain_send2, gain_recv2,
):
    seq, dp = lax.axis_index("seq"), lax.axis_index("dp")
    before = lax.rem(seq + n_seq - 1, n_seq)
    after = lax.rem(seq + 1, n_seq)
    outer = n_seq // inner
    block = lax.div(seq, inner)
    place = lax.rem(seq, inner)
    width = n_dp * 2 * HD

    dp_peers = [(seq, lax.rem(dp + k, n_dp)) for k in range(1, n_dp)]
    in_peers = [(block * inner + lax.rem(place + k, inner), dp) for k in range(1, inner)]
    out_peers = [(lax.rem(block + k, outer) * inner + place, dp) for k in range(1, outer)]
    barrier = pltpu.get_barrier_semaphore()
    peers = [(before, dp), (after, dp)] + dp_peers + in_peers + out_peers
    for peer in peers:
        pl.semaphore_signal(barrier, inc=1, device_id=peer, device_id_type=MESH)

    loads = {}
    for k, (name, src, dst) in enumerate([
        ("eq", eq_h, eq), ("sk", sk_h, sk), ("sv", sv_h, sv), ("ns", ns_h, ns),
        ("sq", sq_h, sq), ("og", og_h, og), ("nk", nk_h, nk), ("gain", gain_h, gain),
    ]):
        loads[name] = pltpu.make_async_copy(src, dst, in_sem.at[k])
        loads[name].start()

    pl.semaphore_wait(barrier, len(peers))

    halo = [
        pltpu.make_async_remote_copy(
            src_ref=src.at[pl.ds(0, SPAN)], dst_ref=dst, send_sem=halo_send.at[k], recv_sem=halo_recv.at[k],
            device_id=(before, dp), device_id_type=MESH)
        for k, (src, dst) in enumerate([(sq_h, next_q), (og_h, next_g)])
    ]
    for copy in halo:
        copy.start()

    left = lax.broadcasted_iota(jnp.int32, (MEM, 2 * SPAN), 1) < SPAN
    tiles = 2 * MEM // 8
    pick = (
        lax.broadcasted_iota(jnp.int32, (tiles, 8, 128), 2)
        == lax.broadcasted_iota(jnp.int32, (tiles, 8, 128), 0)
    )
    pick2 = (
        lax.broadcasted_iota(jnp.int32, (tiles, 8, 128), 2)
        == lax.broadcasted_iota(jnp.int32, (tiles, 8, 128), 0) + tiles
    )

    def fold(x):
        return jnp.sum(x[:, :HD] + x[:, HD:], axis=1, keepdims=True)

    loads["eq"].wait()
    loads["sk"].wait()
    loads["sv"].wait()
    loads["ns"].wait()
    squares = []
    for c in range(2):
        rows = pl.ds(c * MEM, MEM)
        keys = two_heads(sk[pl.ds(c * SPAN, SPAN), :])
        values = two_heads(sv[pl.ds(c * SPAN, SPAN), :])
        e = jnp.exp(nt(eq[rows, :], keys) * SCALE)
        first, last = half_sums(e, left)
        w = e * jnp.where(left, 1.0 / first, 1.0 / last)
        low = w.astype(BF16)
        enc_w[rows, :] = w
        enc_low[rows, :] = low
        x = ns[rows, :].astype(F32) + nn(low, values)
        enc[rows, :] = x
        squares.append(fold(x * x))

    loads["sq"].wait()
    loads["og"].wait()
    loads["nk"].wait()
    loads["gain"].wait()
    gains = gain[...].reshape(1, 2 * HD)
    last_row = lax.broadcasted_iota(jnp.int32, (SPAN, 2 * HD), 0) == SPAN - 1

    def tokens(c):
        if c == 0:
            return (
                jnp.where(last_row, sq[:SPAN, :], sq[SPAN:, :]),
                jnp.where(last_row, og[:SPAN, :], og[SPAN:, :]),
            )
        there = seq < n_seq - 1
        zero = jnp.zeros((SPAN, 2 * HD), BF16)
        return (
            jnp.where(last_row, sq[SPAN:, :], jnp.where(there, next_q[...], zero)),
            jnp.where(last_row, og[SPAN:, :], jnp.where(there, next_g[...], zero)),
        )

    pairs, dots = [], []
    for c in range(2):
        rows = pl.ds(c * MEM, MEM)
        if c == 1:
            for copy in halo:
                copy.wait_recv()
        q, g = tokens(c)
        q, g = two_heads(q), two_heads(g)
        pairs.append((q, g))
        e = jnp.exp(nt(nk[rows, :], q) * SCALE)
        w = e * (1.0 / jnp.sum(e, axis=0, keepdims=True))
        weights[rows, :] = w
        v = nn(w.astype(BF16), g)
        val[rows, :] = v
        dots.append(fold(v * gains * enc[rows, :]))

    def packed(parts, mask):
        whole = jnp.concatenate(parts, axis=0).reshape(tiles, 8, 1)
        return jnp.sum(jnp.where(mask, whole, 0.0), axis=0)

    mine = packed(squares, pick) + packed(dots, pick2)
    part_out[...] = mine
    part = [
        pltpu.make_async_remote_copy(
            src_ref=part_out, dst_ref=part_in.at[k], send_sem=part_send, recv_sem=part_recv,
            device_id=peer, device_id_type=MESH)
        for k, peer in enumerate(dp_peers)
    ]
    for copy in part:
        copy.start()
    pltpu.make_async_copy(part_in, part_in, part_recv).wait()
    totals = mine + jnp.sum(part_in[...], axis=0)
    inverse = lax.rsqrt(totals * (1.0 / width) + NORM_EPS)
    grad_dot = pltpu.roll(totals, tiles, 1)
    slope = grad_dot * inverse * inverse * inverse * (1.0 / width)

    def column(x):
        return jnp.sum(jnp.where(pick, x[None], 0.0), axis=2, keepdims=True).reshape(2 * MEM, 1)

    inverse, slope = column(inverse), column(slope)

    own = jnp.zeros((8, 2 * HD), F32)
    for c in range(2):
        rows = pl.ds(c * MEM, MEM)
        term = val[rows, :] * enc[rows, :] * inverse[c * MEM:(c + 1) * MEM]
        own = own + jnp.sum(term.reshape(MEM // 8, 8, 2 * HD), axis=0)
    own = jnp.sum(own, axis=0, keepdims=True)
    gain_out[...] = jnp.broadcast_to(own, (8, 2 * HD))
    sums = [
        pltpu.make_async_remote_copy(
            src_ref=gain_out, dst_ref=gain_in.at[k], send_sem=gain_send, recv_sem=gain_recv,
            device_id=peer, device_id_type=MESH)
        for k, peer in enumerate(in_peers)
    ]
    for copy in sums:
        copy.start()

    stores = []

    def store(src, dst):
        copy = pltpu.make_async_copy(src, dst, out_sem.at[len(stores)])
        copy.start()
        stores.append(copy)

    d_query = [None, None]
    for c in (1, 0):
        rows = pl.ds(c * MEM, MEM)
        q, g = pairs[c]
        normed = (enc[rows, :] * inverse[c * MEM:(c + 1) * MEM] * gains).astype(BF16)
        w = weights[rows, :]
        d_w = nt(normed, g)
        delta = jnp.sum(w * d_w, axis=0, keepdims=True)
        d_s = (w * (d_w - delta) * SCALE).astype(BF16)
        d_query[c] = diagonal(tn(d_s, nk[rows, :])).astype(BF16)
        if c == 1:
            dq_out[...] = d_query[c]
            back = pltpu.make_async_remote_copy(
                src_ref=dq_out, dst_ref=dq_in, send_sem=back_send, recv_sem=back_recv,
                device_id=(after, dp), device_id_type=MESH)
            back.start()
        kg[rows, :] = nn(d_s, q).astype(BF16)
    store(kg, kg_h)

    pltpu.make_async_copy(gain_in, gain_in, gain_recv).wait()
    own = gain_out[...] + jnp.sum(gain_in[...], axis=0)
    gain_out2[...] = own
    sums2 = [
        pltpu.make_async_remote_copy(
            src_ref=gain_out2, dst_ref=gain_in2.at[k], send_sem=gain_send2, recv_sem=gain_recv2,
            device_id=peer, device_id_type=MESH)
        for k, peer in enumerate(out_peers)
    ]
    for copy in sums2:
        copy.start()

    for c in range(2):
        rows = pl.ds(c * MEM, MEM)
        at = slice(c * MEM, (c + 1) * MEM)
        span = pl.ds(c * SPAN, SPAN)
        keys = two_heads(sk[span, :])
        values = two_heads(sv[span, :])
        s_grad = (inverse[at] * (val[rows, :] * gains) - enc[rows, :] * slope[at]).astype(BF16)
        sg[rows, :] = s_grad
        w = enc_w[rows, :]
        d_w = nt(s_grad, values)
        first, last = half_sums(w * d_w, left)
        d_s = (w * (d_w - jnp.where(left, first, last)) * SCALE).astype(BF16)
        eqg[rows, :] = nn(d_s, keys).astype(BF16)
        skg[span, :] = diagonal(tn(d_s, eq[rows, :])).astype(BF16)
        svg[span, :] = diagonal(tn(enc_low[rows, :], s_grad)).astype(BF16)
    store(sg, sg_h)
    store(eqg, eqg_h)
    store(skg, skg_h)
    store(svg, svg_h)

    pltpu.make_async_copy(gain_in2, gain_in2, gain_recv2).wait()
    own = gain_out2[...] + jnp.sum(gain_in2[...], axis=0)
    gg[...] = own[0:1, :].reshape(2 * HD)
    store(gg, gg_h)

    back.wait_recv()
    come = jnp.where(seq > 0, dq_in[...], jnp.zeros((SPAN, 2 * HD), BF16))
    qg[:SPAN, :] = jnp.where(last_row, d_query[0], come)
    qg[SPAN:, :] = jnp.where(last_row, d_query[1], d_query[0])
    store(qg, qg_h)

    for copy in halo + [back]:
        copy.wait_send()
    for copies, sem in ((part, part_send), (sums, gain_send), (sums2, gain_send2)):
        for copy in copies:
            copy.wait_send()
    for copy in stores:
        copy.wait()


def solution(mesh):
    n_seq, n_dp = mesh.shape["seq"], mesh.shape["dp"]
    inner = 8 if n_seq % 8 == 0 and n_seq > 8 else n_seq // 2
    outer = n_seq // inner

    def step(*args):
        rows, width = args[0].shape
        many = args[2].shape[0]
        small, large = (rows, width), (many, width)
        out_shapes = [small, large, large, large, small, small]
        vmem = pltpu.VMEM
        dma = pltpu.SemaphoreType.DMA
        hbm = pl.BlockSpec(memory_space=pltpu.HBM)
        return pl.pallas_call(
            functools.partial(kernel, n_seq, n_dp, inner),
            out_shape=[jax.ShapeDtypeStruct(s, BF16) for s in out_shapes]
            + [jax.ShapeDtypeStruct((width,), F32)],
            in_specs=[hbm] * 8,
            out_specs=[hbm] * 7,
            scratch_shapes=[
                vmem(small, BF16), vmem(small, BF16), vmem(large, BF16), vmem(large, BF16),
                vmem(large, BF16), vmem(small, BF16), vmem(small, BF16), vmem((width,), F32),
            ]
            + [vmem(s, BF16) for s in out_shapes]
            + [vmem((width,), F32)]
            + [vmem((SPAN, width), BF16)] * 4
            + [
                vmem(large, F32), vmem((many, 2 * SPAN), F32), vmem((many, 2 * SPAN), BF16),
                vmem(large, F32), vmem((many, 2 * SPAN), F32),
                vmem((8, 128), F32), vmem((n_dp - 1, 8, 128), F32),
                vmem((8, width), F32), vmem((inner - 1, 8, width), F32),
                vmem((8, width), F32), vmem((outer - 1, 8, width), F32),
                dma((8,)), dma((7,)), dma((2,)), dma((2,)), dma, dma,
                dma, dma, dma, dma, dma, dma,
            ],
            compiler_params=pltpu.CompilerParams(
                collective_id=0, has_side_effects=True, vmem_limit_bytes=63 * 1024 * 1024
            ),
        )(*args)

    return jax.shard_map(
        step,
        mesh=mesh,
        in_specs=(P("seq", "dp"),) * 7 + (P("dp"),),
        out_specs=(P("seq", "dp"),) * 6 + (P("dp"),),
        check_vma=False,
    )
```

time: 184 us -> 40.5 us (0.22)
  the two profiles are of different devices: /device:TPU:32 before, /device:TPU:1 now
where the time goes in v1:
time: 40.5 us; the launch traced here: 40.2 us
  Pallas kernels  32.4 us (80%)
  local copies, waits for them, and re-layouts  7.17 us (18%)
  between operations  0.65 us (2%)
    pallas_call x1, Pallas kernels, step(): pl.pallas_call(functools.partial(kernel, n_seq, n_dp, inner), out_shape=[...  32.4 us
    unnamed x17, local copies, waits for them, and re-layouts  7.17 us

profile of v1, /device:TPU:1, one launch (start us, length us, event | category | flops | bytes accessed | tf_op | source)
XLA Modules:
  0.0 40.2 jit_solution(7811542286104535912)
XLA Ops:
  0.6 32.4 %shard_map.135 = (bf16[128,256]{1,0:T(8,128)(2,1)}, bf16[512,256]{1,0:T(8,128)(2,1)}, bf16[512,256]{1,0:T(8,128)(2,1)}, bf16[512,256]{1,0:T(8,128)(2,1)}, bf16[1...) custom-call(bf16[128,256]{1,0:T(8,128)(2,1)} %sq_h.1, bf16[128,256]{1,0:T(8,128)(2,1)} %og_h.1, ...), custom_call_target="tpu_custom_call" | custom-call | tf_op jit(solution)/shard_map/pallas_call | solution.py:296
  33.0 1.5 %copy.22 = bf16[128,256]{1,0:T(8,128)(2,1)} copy(bf16[128,256]{1,0:T(8,128)(2,1)} %get-tuple-element.14) | data formatting | bytes 131072
  34.5 0.0 copy-start.1
  34.5 1.7 %copy.23 = bf16[512,256]{1,0:T(8,128)(2,1)} copy(bf16[512,256]{1,0:T(8,128)(2,1)} %get-tuple-element.15) | data formatting | bytes 524288
  36.2 0.0 copy-done.1
  36.2 0.0 copy-start
  36.2 0.7 %copy.24 = bf16[512,256]{1,0:T(8,128)(2,1)} copy(bf16[512,256]{1,0:T(8,128)(2,1)S(1)} %copy-done.1) | data formatting | bytes 524288
  36.9 0.3 copy-done
  37.2 0.0 copy-start.3
  37.2 0.7 %copy.25 = bf16[512,256]{1,0:T(8,128)(2,1)} copy(bf16[512,256]{1,0:T(8,128)(2,1)S(1)} %copy-done) | data formatting | bytes 524288
  37.9 0.2 copy-done.3
  38.1 0.0 copy-start.2
  38.1 0.6 %copy.26 = bf16[128,256]{1,0:T(8,128)(2,1)} copy(bf16[128,256]{1,0:T(8,128)(2,1)S(1)} %copy-done.3) | data formatting | bytes 131072
  38.7 0.2 copy-done.2
  39.0 0.0 copy-start.4
  39.0 0.6 %copy.27 = bf16[128,256]{1,0:T(8,128)(2,1)} copy(bf16[128,256]{1,0:T(8,128)(2,1)S(1)} %copy-done.2) | data formatting | bytes 131072
  39.6 0.0 copy-done.4
  39.6 0.6 %copy.28 = f32[256]{0:T(256)} copy(f32[256]{0:T(256)S(1)} %copy-done.4) | data formatting | bytes 2048
Async XLA Ops:
  34.5 1.7 %copy-start.1 = (bf16[512,256]{1,0:T(8,128)(2,1)S(1)}, bf16[512,256]{1,0:T(8,128)(2,1)}, u32[]{:S(2)}) copy-start(bf16[512,256]{1,0:T(8,128)(2,1)} %get-tuple-element.16) | copy-start | bytes 786436
  36.2 1.0 %copy-start = (bf16[512,256]{1,0:T(8,128)(2,1)S(1)}, bf16[512,256]{1,0:T(8,128)(2,1)}, u32[]{:S(2)}) copy-start(bf16[512,256]{1,0:T(8,128)(2,1)} %get-tuple-element.17) | copy-start | bytes 786436
  37.2 0.9 %copy-start.3 = (bf16[128,256]{1,0:T(8,128)(2,1)S(1)}, bf16[128,256]{1,0:T(8,128)(2,1)}, u32[]{:S(2)}) copy-start(bf16[128,256]{1,0:T(8,128)(2,1)} %get-tuple-element.18) | copy-start | bytes 196612
  38.1 0.9 %copy-start.2 = (bf16[128,256]{1,0:T(8,128)(2,1)S(1)}, bf16[128,256]{1,0:T(8,128)(2,1)}, u32[]{:S(2)}) copy-start(bf16[128,256]{1,0:T(8,128)(2,1)} %get-tuple-element.19) | copy-start | bytes 196612
  39.0 0.7 %copy-start.4 = (f32[256]{0:T(256)S(1)}, f32[256]{0:T(256)}, u32[]{:S(2)}) copy-start(f32[256]{0:T(256)} %get-tuple-element.20) | copy-start | bytes 3076

commit v2 on v1

--- a/solution.py
+++ b/solution.py
@@ -49,12 +49,11 @@
 
 def kernel(
     n_seq, n_dp, inner, sq_h, og_h, nk_h, ns_h, eq_h, sk_h, sv_h, gain_h,
-    qg_h, kg_h, sg_h, eqg_h, skg_h, svg_h, gg_h,
+    qg, kg, sg, eqg, skg, svg, gg,
     sq, og, nk, ns, eq, sk, sv, gain,
-    qg, kg, sg, eqg, skg, svg, gg,
     next_q, next_g, dq_out, dq_in, enc, enc_w, enc_low, val, weights,
     part_out, part_in, gain_out, gain_in, gain_out2, gain_in2,
-    in_sem, out_sem, halo_send, halo_recv, back_send, back_recv,
+    in_sem, halo_send, halo_recv, back_send, back_recv,
     part_send, part_recv, gain_send, gain_recv, gain_send2, gain_recv2,
 ):
     seq, dp = lax.axis_index("seq"), lax.axis_index("dp")
@@ -201,13 +200,6 @@
     ]
     for copy in sums:
         copy.start()
-
-    stores = []
-
-    def store(src, dst):
-        copy = pltpu.make_async_copy(src, dst, out_sem.at[len(stores)])
-        copy.start()
-        stores.append(copy)
 
     d_query = [None, None]
     for c in (1, 0):
@@ -226,7 +218,6 @@
                 device_id=(after, dp), device_id_type=MESH)
             back.start()
         kg[rows, :] = nn(d_s, q).astype(BF16)
-    store(kg, kg_h)
 
     pltpu.make_async_copy(gain_in, gain_in, gain_recv).wait()
     own = gain_out[...] + jnp.sum(gain_in[...], axis=0)
@@ -255,28 +246,28 @@
         eqg[rows, :] = nn(d_s, keys).astype(BF16)
         skg[span, :] = diagonal(tn(d_s, eq[rows, :])).astype(BF16)
         svg[span, :] = diagonal(tn(enc_low[rows, :], s_grad)).astype(BF16)
-    store(sg, sg_h)
-    store(eqg, eqg_h)
-    store(skg, skg_h)
-    store(svg, svg_h)
 
     pltpu.make_async_copy(gain_in2, gain_in2, gain_recv2).wait()
     own = gain_out2[...] + jnp.sum(gain_in2[...], axis=0)
     gg[...] = own[0:1, :].reshape(2 * HD)
-    store(gg, gg_h)
 
     back.wait_recv()
     come = jnp.where(seq > 0, dq_in[...], jnp.zeros((SPAN, 2 * HD), BF16))
     qg[:SPAN, :] = jnp.where(last_row, d_query[0], come)
     qg[SPAN:, :] = jnp.where(last_row, d_query[1], d_query[0])
-    store(qg, qg_h)
 
     for copy in halo + [back]:
         copy.wait_send()
-    for copies, sem in ((part, part_send), (sums, gain_send), (sums2, gain_send2)):
-        for copy in copies:
-            copy.wait_send()
-    for copy in stores:
+    for copy in part + sums + sums2:
+        copy.wait_send()
+
+
+def write_back(*refs):
+    sources, targets, sem = refs[:7], refs[7:14], refs[14]
+    copies = [pltpu.make_async_copy(a, b, sem.at[k]) for k, (a, b) in enumerate(zip(sources, targets))]
+    for copy in copies:
+        copy.start()
+    for copy in copies:
         copy.wait()
 
 
@@ -293,18 +284,16 @@
         vmem = pltpu.VMEM
         dma = pltpu.SemaphoreType.DMA
         hbm = pl.BlockSpec(memory_space=pltpu.HBM)
-        return pl.pallas_call(
+        on_chip = pl.BlockSpec(memory_space=pltpu.VMEM)
+        results = pl.pallas_call(
             functools.partial(kernel, n_seq, n_dp, inner),
-            out_shape=[jax.ShapeDtypeStruct(s, BF16) for s in out_shapes]
-            + [jax.ShapeDtypeStruct((width,), F32)],
+            out_shape=[vmem(s, BF16) for s in out_shapes] + [vmem((width,), F32)],
             in_specs=[hbm] * 8,
-            out_specs=[hbm] * 7,
+            out_specs=[on_chip] * 7,
             scratch_shapes=[
                 vmem(small, BF16), vmem(small, BF16), vmem(large, BF16), vmem(large, BF16),
                 vmem(large, BF16), vmem(small, BF16), vmem(small, BF16), vmem((width,), F32),
             ]
-            + [vmem(s, BF16) for s in out_shapes]
-            + [vmem((width,), F32)]
             + [vmem((SPAN, width), BF16)] * 4
             + [
                 vmem(large, F32), vmem((many, 2 * SPAN), F32), vmem((many, 2 * SPAN), BF16),
@@ -312,13 +301,21 @@
                 vmem((8, 128), F32), vmem((n_dp - 1, 8, 128), F32),
                 vmem((8, width), F32), vmem((inner - 1, 8, width), F32),
                 vmem((8, width), F32), vmem((outer - 1, 8, width), F32),
-                dma((8,)), dma((7,)), dma((2,)), dma((2,)), dma, dma,
+                dma((8,)), dma((2,)), dma((2,)), dma, dma,
                 dma, dma, dma, dma, dma, dma,
             ],
             compiler_params=pltpu.CompilerParams(
-                collective_id=0, has_side_effects=True, vmem_limit_bytes=63 * 1024 * 1024
+                collective_id=0, has_side_effects=True, vmem_limit_bytes=58 * 1024 * 1024
             ),
         )(*args)
+        return pl.pallas_call(
+            write_back,
+            out_shape=[jax.ShapeDtypeStruct(s, BF16) for s in out_shapes]
+            + [jax.ShapeDtypeStruct((width,), F32)],
+            in_specs=[pl.BlockSpec(memory_space=pl.ANY)] * 7,
+            out_specs=[hbm] * 7,
+            scratch_shapes=[dma((7,))],
+        )(*[pltpu.with_memory_space_constraint(x, pltpu.VMEM) for x in results])
 
     return jax.shard_map(
         step,

time: 40.5 us -> 33.4 us (0.82)
  local copies, waits for them, and re-layouts: 7.17 us -> 0 us
    unnamed x17 -> x0, local copies, waits for them, and re-layouts: 7.17 us -> none
    pallas_call x0 -> x1, Pallas kernels: none -> 1 us  [step(): pl.pallas_call(write_back, out_shape=[jax.ShapeDtypeStruct(s, BF16) for s...]
    pallas_call x1, Pallas kernels: 32.4 us -> 31.7 us  [step(): pl.pallas_call(functools.partial(kernel, n_seq, n_dp, inner), out_shape=[...]
where the time goes in v2:
time: 33.4 us; the launch traced here: 33.3 us
  Pallas kernels  32.7 us (98%)
  between operations  0.64 us (2%)
    pallas_call x1, Pallas kernels, step(): pl.pallas_call(functools.partial(kernel, n_seq, n_dp, inner), out_shape=[...  31.7 us
    pallas_call x1, Pallas kernels, step(): pl.pallas_call(write_back, out_shape=[jax.ShapeDtypeStruct(s, BF16) for s...  1 us

profile of v2, /device:TPU:1, one launch (start us, length us, event | category | flops | bytes accessed | tf_op | source)
XLA Modules:
  0.0 33.3 jit_solution(5480233360582887294)
XLA Ops:
  0.6 31.7 %shard_map.135 = (bf16[128,256]{1,0:T(8,128)(2,1)S(1)}, bf16[512,256]{1,0:T(8,128)(2,1)S(1)}, bf16[512,256]{1,0:T(8,128)(2,1)S(1)}, bf16[512,256]{1,0:T(8,128)(2...) custom-call(bf16[128,256]{1,0:T(8,128)(2,1)} %sq_h.1, bf16[128,256]{1,0:T(8,128)(2,1)} %og_h.1, ...), custom_call_target="tpu_custom_call" | custom-call | tf_op jit(solution)/shard_map/pallas_call | solution.py:288
  32.3 1.0 %shard_map.136 = (bf16[128,256]{1,0:T(8,128)(2,1)}, bf16[512,256]{1,0:T(8,128)(2,1)}, bf16[512,256]{1,0:T(8,128)(2,1)}, bf16[512,256]{1,0:T(8,128)(2,1)}, bf16[1...) custom-call(bf16[128,256]{1,0:T(8,128)(2,1)S(1)} %get-tuple-element.14.refs_0_, ...), custom_call_target="tpu_custom_call" | custom-call | tf_op jit(solution)/shard_map/pallas_call | solution.py:311

commit v3 on v2

--- a/solution.py
+++ b/solution.py
@@ -52,9 +52,9 @@
     qg, kg, sg, eqg, skg, svg, gg,
     sq, og, nk, ns, eq, sk, sv, gain,
     next_q, next_g, dq_out, dq_in, enc, enc_w, enc_low, val, weights,
-    part_out, part_in, gain_out, gain_in, gain_out2, gain_in2,
+    square_out, square_in, dot_out, dot_in, gain_out, gain_in, gain_out2, gain_in2,
     in_sem, halo_send, halo_recv, back_send, back_recv,
-    part_send, part_recv, gain_send, gain_recv, gain_send2, gain_recv2,
+    square_send, square_recv, dot_send, dot_recv, gain_send, gain_recv, gain_send2, gain_recv2,
 ):
     seq, dp = lax.axis_index("seq"), lax.axis_index("dp")
     before = lax.rem(seq + n_seq - 1, n_seq)
@@ -64,11 +64,12 @@
     place = lax.rem(seq, inner)
     width = n_dp * 2 * HD
 
-    dp_peers = [(seq, lax.rem(dp + k, n_dp)) for k in range(1, n_dp)]
+    far = sorted(range(1, n_dp), key=lambda k: -min(k, n_dp - k))
+    dp_peers = [(seq, lax.rem(dp + k, n_dp)) for k in far]
     in_peers = [(block * inner + lax.rem(place + k, inner), dp) for k in range(1, inner)]
     out_peers = [(lax.rem(block + k, outer) * inner + place, dp) for k in range(1, outer)]
     barrier = pltpu.get_barrier_semaphore()
-    peers = [(before, dp), (after, dp)] + dp_peers + in_peers + out_peers
+    peers = [(before, dp), (after, dp)] + dp_peers + out_peers + in_peers
     for peer in peers:
         pl.semaphore_signal(barrier, inc=1, device_id=peer, device_id_type=MESH)
 
@@ -80,28 +81,12 @@
         loads[name] = pltpu.make_async_copy(src, dst, in_sem.at[k])
         loads[name].start()
 
-    pl.semaphore_wait(barrier, len(peers))
-
-    halo = [
-        pltpu.make_async_remote_copy(
-            src_ref=src.at[pl.ds(0, SPAN)], dst_ref=dst, send_sem=halo_send.at[k], recv_sem=halo_recv.at[k],
-            device_id=(before, dp), device_id_type=MESH)
-        for k, (src, dst) in enumerate([(sq_h, next_q), (og_h, next_g)])
-    ]
-    for copy in halo:
-        copy.start()
-
     left = lax.broadcasted_iota(jnp.int32, (MEM, 2 * SPAN), 1) < SPAN
     tiles = 2 * MEM // 8
     pick = (
         lax.broadcasted_iota(jnp.int32, (tiles, 8, 128), 2)
         == lax.broadcasted_iota(jnp.int32, (tiles, 8, 128), 0)
     )
-    pick2 = (
-        lax.broadcasted_iota(jnp.int32, (tiles, 8, 128), 2)
-        == lax.broadcasted_iota(jnp.int32, (tiles, 8, 128), 0) + tiles
-    )
-
     def fold(x):
         return jnp.sum(x[:, :HD] + x[:, HD:], axis=1, keepdims=True)
 
@@ -123,6 +108,43 @@
         x = ns[rows, :].astype(F32) + nn(low, values)
         enc[rows, :] = x
         squares.append(fold(x * x))
+
+    def packed(parts):
+        whole = jnp.concatenate(parts, axis=0).reshape(tiles, 8, 1)
+        return jnp.sum(jnp.where(pick, whole, 0.0), axis=0)
+
+    def column(x):
+        return jnp.sum(jnp.where(pick, x[None], 0.0), axis=2, keepdims=True).reshape(2 * MEM, 1)
+
+    def exchange(mine, out, into, send, recv):
+        out[...] = mine
+        copies = [
+            pltpu.make_async_remote_copy(
+                src_ref=out, dst_ref=into.at[k], send_sem=send, recv_sem=recv,
+                device_id=peer, device_id_type=MESH)
+            for k, peer in enumerate(dp_peers)
+        ]
+        for copy in copies:
+            copy.start()
+        return copies
+
+    def gather(out, into, recv):
+        pltpu.make_async_copy(into, into, recv).wait()
+        return out[...] + jnp.sum(into[...], axis=0)
+
+    squares = packed(squares)
+    pl.semaphore_wait(barrier, len(peers))
+
+    halo = [
+        pltpu.make_async_remote_copy(
+            src_ref=src.at[pl.ds(0, SPAN)], dst_ref=dst, send_sem=halo_send.at[k], recv_sem=halo_recv.at[k],
+            device_id=(before, dp), device_id_type=MESH)
+        for k, (src, dst) in enumerate([(sq_h, next_q), (og_h, next_g)])
+    ]
+    for copy in halo:
+        copy.start()
+
+    send_squares = exchange(squares, square_out, square_in, square_send, square_recv)
 
     loads["sq"].wait()
     loads["og"].wait()
@@ -160,30 +182,10 @@
         val[rows, :] = v
         dots.append(fold(v * gains * enc[rows, :]))
 
-    def packed(parts, mask):
-        whole = jnp.concatenate(parts, axis=0).reshape(tiles, 8, 1)
-        return jnp.sum(jnp.where(mask, whole, 0.0), axis=0)
-
-    mine = packed(squares, pick) + packed(dots, pick2)
-    part_out[...] = mine
-    part = [
-        pltpu.make_async_remote_copy(
-            src_ref=part_out, dst_ref=part_in.at[k], send_sem=part_send, recv_sem=part_recv,
-            device_id=peer, device_id_type=MESH)
-        for k, peer in enumerate(dp_peers)
-    ]
-    for copy in part:
-        copy.start()
-    pltpu.make_async_copy(part_in, part_in, part_recv).wait()
-    totals = mine + jnp.sum(part_in[...], axis=0)
-    inverse = lax.rsqrt(totals * (1.0 / width) + NORM_EPS)
-    grad_dot = pltpu.roll(totals, tiles, 1)
-    slope = grad_dot * inverse * inverse * inverse * (1.0 / width)
-
-    def column(x):
-        return jnp.sum(jnp.where(pick, x[None], 0.0), axis=2, keepdims=True).reshape(2 * MEM, 1)
-
-    inverse, slope = column(inverse), column(slope)
+    send_dots = exchange(packed(dots), dot_out, dot_in, dot_send, dot_recv)
+    inverse = lax.rsqrt(gather(square_out, square_in, square_recv) * (1.0 / width) + NORM_EPS)
+    packed_inverse = inverse
+    inverse = column(inverse)
 
     own = jnp.zeros((8, 2 * HD), F32)
     for c in range(2):
@@ -231,6 +233,8 @@
     for copy in sums2:
         copy.start()
 
+    grad_dot = gather(dot_out, dot_in, dot_recv)
+    slope = column(grad_dot * packed_inverse * packed_inverse * packed_inverse * (1.0 / width))
     for c in range(2):
         rows = pl.ds(c * MEM, MEM)
         at = slice(c * MEM, (c + 1) * MEM)
@@ -258,7 +262,7 @@
 
     for copy in halo + [back]:
         copy.wait_send()
-    for copy in part + sums + sums2:
+    for copy in send_squares + send_dots + sums + sums2:
         copy.wait_send()
 
 
@@ -299,10 +303,11 @@
                 vmem(large, F32), vmem((many, 2 * SPAN), F32), vmem((many, 2 * SPAN), BF16),
                 vmem(large, F32), vmem((many, 2 * SPAN), F32),
                 vmem((8, 128), F32), vmem((n_dp - 1, 8, 128), F32),
+                vmem((8, 128), F32), vmem((n_dp - 1, 8, 128), F32),
                 vmem((8, width), F32), vmem((inner - 1, 8, width), F32),
                 vmem((8, width), F32), vmem((outer - 1, 8, width), F32),
                 dma((8,)), dma((2,)), dma((2,)), dma, dma,
-                dma, dma, dma, dma, dma, dma,
+                dma, dma, dma, dma, dma, dma, dma, dma,
             ],
             compiler_params=pltpu.CompilerParams(
                 collective_id=0, has_side_effects=True, vmem_limit_bytes=58 * 1024 * 1024

time: 33.4 us -> 30.6 us (0.916)
  Pallas kernels: 32.7 us -> 29.8 us
    pallas_call x1, Pallas kernels: 31.7 us -> 28.8 us  [step(): pl.pallas_call(functools.partial(kernel, n_seq, n_dp, inner), out_shape=[...]
where the time goes in v3:
time: 30.6 us; the launch traced here: 30.5 us
  Pallas kernels  29.8 us (97%)
  between operations  0.64 us (2%)
    pallas_call x1, Pallas kernels, step(): pl.pallas_call(functools.partial(kernel, n_seq, n_dp, inner), out_shape=[...  28.8 us
    pallas_call x1, Pallas kernels, step(): pl.pallas_call(write_back, out_shape=[jax.ShapeDtypeStruct(s, BF16) for s...  1 us

profile of v3, /device:TPU:1, one launch (start us, length us, event | category | flops | bytes accessed | tf_op | source)
XLA Modules:
  0.0 30.5 jit_solution(15548421841015244105)
XLA Ops:
  0.6 28.8 %shard_map.135 = (bf16[128,256]{1,0:T(8,128)(2,1)S(1)}, bf16[512,256]{1,0:T(8,128)(2,1)S(1)}, bf16[512,256]{1,0:T(8,128)(2,1)S(1)}, bf16[512,256]{1,0:T(8,128)(2...) custom-call(bf16[128,256]{1,0:T(8,128)(2,1)} %sq_h.1, bf16[128,256]{1,0:T(8,128)(2,1)} %og_h.1, ...), custom_call_target="tpu_custom_call" | custom-call | tf_op jit(solution)/shard_map/pallas_call | solution.py:292
  29.5 1.0 %shard_map.136 = (bf16[128,256]{1,0:T(8,128)(2,1)}, bf16[512,256]{1,0:T(8,128)(2,1)}, bf16[512,256]{1,0:T(8,128)(2,1)}, bf16[512,256]{1,0:T(8,128)(2,1)}, bf16[1...) custom-call(bf16[128,256]{1,0:T(8,128)(2,1)S(1)} %get-tuple-element.14.refs_0_, ...), custom_call_target="tpu_custom_call" | custom-call | tf_op jit(solution)/shard_map/pallas_call | solution.py:316

commit v4 on v3

--- a/solution.py
+++ b/solution.py
@@ -48,30 +48,30 @@
 
 
 def kernel(
-    n_seq, n_dp, inner, sq_h, og_h, nk_h, ns_h, eq_h, sk_h, sv_h, gain_h,
+    n_seq, n_dp, split, sq_h, og_h, nk_h, ns_h, eq_h, sk_h, sv_h, gain_h,
     qg, kg, sg, eqg, skg, svg, gg,
     sq, og, nk, ns, eq, sk, sv, gain,
     next_q, next_g, dq_out, dq_in, enc, enc_w, enc_low, val, weights,
-    square_out, square_in, dot_out, dot_in, gain_out, gain_in, gain_out2, gain_in2,
+    square_out, square_in, dot_out, dot_in, gain_out, gain_in,
     in_sem, halo_send, halo_recv, back_send, back_recv,
-    square_send, square_recv, dot_send, dot_recv, gain_send, gain_recv, gain_send2, gain_recv2,
+    square_send, square_recv, dot_send, dot_recv, gain_send, gain_recv,
 ):
     seq, dp = lax.axis_index("seq"), lax.axis_index("dp")
     before = lax.rem(seq + n_seq - 1, n_seq)
     after = lax.rem(seq + 1, n_seq)
-    outer = n_seq // inner
-    block = lax.div(seq, inner)
-    place = lax.rem(seq, inner)
     width = n_dp * 2 * HD
 
     far = sorted(range(1, n_dp), key=lambda k: -min(k, n_dp - k))
     dp_peers = [(seq, lax.rem(dp + k, n_dp)) for k in far]
-    in_peers = [(block * inner + lax.rem(place + k, inner), dp) for k in range(1, inner)]
-    out_peers = [(lax.rem(block + k, outer) * inner + place, dp) for k in range(1, outer)]
-    barrier = pltpu.get_barrier_semaphore()
-    peers = [(before, dp), (after, dp)] + dp_peers + out_peers + in_peers
-    for peer in peers:
-        pl.semaphore_signal(barrier, inc=1, device_id=peer, device_id_type=MESH)
+    b_size, x_size, c_size = split
+    block, rest = lax.div(seq, x_size * c_size), lax.rem(seq, x_size * c_size)
+    across, core = lax.div(rest, c_size), lax.rem(rest, c_size)
+    offsets = [(i, j, k) for i in range(b_size) for j in range(x_size) for k in range(c_size)][1:]
+    offsets.sort(key=lambda o: -(4 * min(o[0], b_size - o[0]) + 2 * min(o[1], x_size - o[1]) + o[2]))
+    seq_peers = [
+        (lax.rem(block + i, b_size) * (x_size * c_size) + lax.rem(across + j, x_size) * c_size + lax.rem(core + k, c_size), dp)
+        for i, j, k in offsets
+    ]
 
     loads = {}
     for k, (name, src, dst) in enumerate([
@@ -80,6 +80,11 @@
     ]):
         loads[name] = pltpu.make_async_copy(src, dst, in_sem.at[k])
         loads[name].start()
+
+    barrier = pltpu.get_barrier_semaphore()
+    peers = seq_peers + dp_peers
+    for peer in peers:
+        pl.semaphore_signal(barrier, inc=1, device_id=peer, device_id_type=MESH)
 
     left = lax.broadcasted_iota(jnp.int32, (MEM, 2 * SPAN), 1) < SPAN
     tiles = 2 * MEM // 8
@@ -126,7 +131,6 @@
         ]
         for copy in copies:
             copy.start()
-        return copies
 
     def gather(out, into, recv):
         pltpu.make_async_copy(into, into, recv).wait()
@@ -144,7 +148,7 @@
     for copy in halo:
         copy.start()
 
-    send_squares = exchange(squares, square_out, square_in, square_send, square_recv)
+    exchange(squares, square_out, square_in, square_send, square_recv)
 
     loads["sq"].wait()
     loads["og"].wait()
@@ -182,7 +186,7 @@
         val[rows, :] = v
         dots.append(fold(v * gains * enc[rows, :]))
 
-    send_dots = exchange(packed(dots), dot_out, dot_in, dot_send, dot_recv)
+    exchange(packed(dots), dot_out, dot_in, dot_send, dot_recv)
     inverse = lax.rsqrt(gather(square_out, square_in, square_recv) * (1.0 / width) + NORM_EPS)
     packed_inverse = inverse
     inverse = column(inverse)
@@ -193,12 +197,12 @@
         term = val[rows, :] * enc[rows, :] * inverse[c * MEM:(c + 1) * MEM]
         own = own + jnp.sum(term.reshape(MEM // 8, 8, 2 * HD), axis=0)
     own = jnp.sum(own, axis=0, keepdims=True)
-    gain_out[...] = jnp.broadcast_to(own, (8, 2 * HD))
+    gain_out[...] = jnp.concatenate([own[:, :HD], own[:, HD:]], axis=0)
     sums = [
         pltpu.make_async_remote_copy(
             src_ref=gain_out, dst_ref=gain_in.at[k], send_sem=gain_send, recv_sem=gain_recv,
             device_id=peer, device_id_type=MESH)
-        for k, peer in enumerate(in_peers)
+        for k, peer in enumerate(seq_peers)
     ]
     for copy in sums:
         copy.start()
@@ -221,18 +225,6 @@
             back.start()
         kg[rows, :] = nn(d_s, q).astype(BF16)
 
-    pltpu.make_async_copy(gain_in, gain_in, gain_recv).wait()
-    own = gain_out[...] + jnp.sum(gain_in[...], axis=0)
-    gain_out2[...] = own
-    sums2 = [
-        pltpu.make_async_remote_copy(
-            src_ref=gain_out2, dst_ref=gain_in2.at[k], send_sem=gain_send2, recv_sem=gain_recv2,
-            device_id=peer, device_id_type=MESH)
-        for k, peer in enumerate(out_peers)
-    ]
-    for copy in sums2:
-        copy.start()
-
     grad_dot = gather(dot_out, dot_in, dot_recv)
     slope = column(grad_dot * packed_inverse * packed_inverse * packed_inverse * (1.0 / width))
     for c in range(2):
@@ -251,10 +243,6 @@
         skg[span, :] = diagonal(tn(d_s, eq[rows, :])).astype(BF16)
         svg[span, :] = diagonal(tn(enc_low[rows, :], s_grad)).astype(BF16)
 
-    pltpu.make_async_copy(gain_in2, gain_in2, gain_recv2).wait()
-    own = gain_out2[...] + jnp.sum(gain_in2[...], axis=0)
-    gg[...] = own[0:1, :].reshape(2 * HD)
-
     back.wait_recv()
     come = jnp.where(seq > 0, dq_in[...], jnp.zeros((SPAN, 2 * HD), BF16))
     qg[:SPAN, :] = jnp.where(last_row, d_query[0], come)
@@ -262,8 +250,11 @@
 
     for copy in halo + [back]:
         copy.wait_send()
-    for copy in send_squares + send_dots + sums + sums2:
-        copy.wait_send()
+    for slots, sem in ((square_in, square_send), (dot_in, dot_send), (gain_in, gain_send)):
+        pltpu.make_async_copy(slots, slots, sem).wait()
+
+    total = gather(gain_out, gain_in, gain_recv)
+    gg[...] = jnp.concatenate([total[0:1], total[1:2]], axis=1).reshape(2 * HD)
 
 
 def write_back(*refs):
@@ -277,8 +268,8 @@
 
 def solution(mesh):
     n_seq, n_dp = mesh.shape["seq"], mesh.shape["dp"]
-    inner = 8 if n_seq % 8 == 0 and n_seq > 8 else n_seq // 2
-    outer = n_seq // inner
+    across = min(4, n_seq // 4)
+    split = (n_seq // (2 * across), across, 2)
 
     def step(*args):
         rows, width = args[0].shape
@@ -290,7 +281,7 @@
         hbm = pl.BlockSpec(memory_space=pltpu.HBM)
         on_chip = pl.BlockSpec(memory_space=pltpu.VMEM)
         results = pl.pallas_call(
-            functools.partial(kernel, n_seq, n_dp, inner),
+            functools.partial(kernel, n_seq, n_dp, split),
             out_shape=[vmem(s, BF16) for s in out_shapes] + [vmem((width,), F32)],
             in_specs=[hbm] * 8,
             out_specs=[on_chip] * 7,
@@ -304,10 +295,9 @@
                 vmem(large, F32), vmem((many, 2 * SPAN), F32),
                 vmem((8, 128), F32), vmem((n_dp - 1, 8, 128), F32),
                 vmem((8, 128), F32), vmem((n_dp - 1, 8, 128), F32),
-                vmem((8, width), F32), vmem((inner - 1, 8, width), F32),
-                vmem((8, width), F32), vmem((outer - 1, 8, width), F32),
+                vmem((2, HD), F32), vmem((n_seq - 1, 2, HD), F32),
                 dma((8,)), dma((2,)), dma((2,)), dma, dma,
-                dma, dma, dma, dma, dma, dma, dma, dma,
+                dma, dma, dma, dma, dma, dma,
             ],
             compiler_params=pltpu.CompilerParams(
                 collective_id=0, has_side_effects=True, vmem_limit_bytes=58 * 1024 * 1024

time: 30.6 us -> 28.8 us (0.941)
  Pallas kernels: 29.8 us -> 28 us
    pallas_call x1, Pallas kernels: 28.8 us -> 27 us  [step(): pl.pallas_call(functools.partial(kernel, n_seq, n_dp, split), out_shape=[...]
where the time goes in v4:
time: 28.8 us; the launch traced here: 28.7 us
  Pallas kernels  28 us (97%)
  between operations  0.64 us (2%)
    pallas_call x1, Pallas kernels, step(): pl.pallas_call(functools.partial(kernel, n_seq, n_dp, split), out_shape=[...  27 us
    pallas_call x1, Pallas kernels, step(): pl.pallas_call(write_back, out_shape=[jax.ShapeDtypeStruct(s, BF16) for s...  1 us

profile of v4, /device:TPU:1, one launch (start us, length us, event | category | flops | bytes accessed | tf_op | source)
XLA Modules:
  0.0 28.7 jit_solution(3005804224127270732)
XLA Ops:
  0.6 27.0 %shard_map.135 = (bf16[128,256]{1,0:T(8,128)(2,1)S(1)}, bf16[512,256]{1,0:T(8,128)(2,1)S(1)}, bf16[512,256]{1,0:T(8,128)(2,1)S(1)}, bf16[512,256]{1,0:T(8,128)(2...) custom-call(bf16[128,256]{1,0:T(8,128)(2,1)} %sq_h.1, bf16[128,256]{1,0:T(8,128)(2,1)} %og_h.1, ...), custom_call_target="tpu_custom_call" | custom-call | tf_op jit(solution)/shard_map/pallas_call | solution.py:283
  27.7 1.0 %shard_map.136 = (bf16[128,256]{1,0:T(8,128)(2,1)}, bf16[512,256]{1,0:T(8,128)(2,1)}, bf16[512,256]{1,0:T(8,128)(2,1)}, bf16[512,256]{1,0:T(8,128)(2,1)}, bf16[1...) custom-call(bf16[128,256]{1,0:T(8,128)(2,1)S(1)} %get-tuple-element.14.refs_0_, ...), custom_call_target="tpu_custom_call" | custom-call | tf_op jit(solution)/shard_map/pallas_call | solution.py:306

commit v5 on v4

--- a/solution.py
+++ b/solution.py
@@ -48,7 +48,7 @@
 
 
 def kernel(
-    n_seq, n_dp, split, sq_h, og_h, nk_h, ns_h, eq_h, sk_h, sv_h, gain_h,
+    n_seq, n_dp, sq_h, og_h, nk_h, ns_h, eq_h, sk_h, sv_h, gain_h,
     qg, kg, sg, eqg, skg, svg, gg,
     sq, og, nk, ns, eq, sk, sv, gain,
     next_q, next_g, dq_out, dq_in, enc, enc_w, enc_low, val, weights,
@@ -61,17 +61,15 @@
     after = lax.rem(seq + 1, n_seq)
     width = n_dp * 2 * HD
 
-    far = sorted(range(1, n_dp), key=lambda k: -min(k, n_dp - k))
-    dp_peers = [(seq, lax.rem(dp + k, n_dp)) for k in far]
-    b_size, x_size, c_size = split
-    block, rest = lax.div(seq, x_size * c_size), lax.rem(seq, x_size * c_size)
-    across, core = lax.div(rest, c_size), lax.rem(rest, c_size)
-    offsets = [(i, j, k) for i in range(b_size) for j in range(x_size) for k in range(c_size)][1:]
-    offsets.sort(key=lambda o: -(4 * min(o[0], b_size - o[0]) + 2 * min(o[1], x_size - o[1]) + o[2]))
-    seq_peers = [
-        (lax.rem(block + i, b_size) * (x_size * c_size) + lax.rem(across + j, x_size) * c_size + lax.rem(core + k, c_size), dp)
-        for i, j, k in offsets
-    ]
+    def falling(me, n):
+        return [n - 1 - k - lax.div(me + k + 1, n) for k in range(n - 1)]
+
+    def rising(me, n):
+        above = [lax.div(me - k + n - 1, n) for k in range(n - 1)]
+        return [(k + 1 - up, me - up) for k, up in enumerate(above)]
+
+    dp_peers = [((seq, peer), slot) for peer, slot in rising(dp, n_dp)]
+    seq_peers = [((peer, dp), slot) for peer, slot in rising(seq, n_seq)]
 
     loads = {}
     for k, (name, src, dst) in enumerate([
@@ -82,7 +80,7 @@
         loads[name].start()
 
     barrier = pltpu.get_barrier_semaphore()
-    peers = seq_peers + dp_peers
+    peers = [(seq, peer) for peer in falling(dp, n_dp)] + [(peer, dp) for peer in falling(seq, n_seq)]
     for peer in peers:
         pl.semaphore_signal(barrier, inc=1, device_id=peer, device_id_type=MESH)
 
@@ -125,9 +123,9 @@
         out[...] = mine
         copies = [
             pltpu.make_async_remote_copy(
-                src_ref=out, dst_ref=into.at[k], send_sem=send, recv_sem=recv,
+                src_ref=out, dst_ref=into.at[slot], send_sem=send, recv_sem=recv,
                 device_id=peer, device_id_type=MESH)
-            for k, peer in enumerate(dp_peers)
+            for peer, slot in dp_peers
         ]
         for copy in copies:
             copy.start()
@@ -200,9 +198,9 @@
     gain_out[...] = jnp.concatenate([own[:, :HD], own[:, HD:]], axis=0)
     sums = [
         pltpu.make_async_remote_copy(
-            src_ref=gain_out, dst_ref=gain_in.at[k], send_sem=gain_send, recv_sem=gain_recv,
+            src_ref=gain_out, dst_ref=gain_in.at[slot], send_sem=gain_send, recv_sem=gain_recv,
             device_id=peer, device_id_type=MESH)
-        for k, peer in enumerate(seq_peers)
+        for peer, slot in seq_peers
     ]
     for copy in sums:
         copy.start()
@@ -268,9 +266,6 @@
 
 def solution(mesh):
     n_seq, n_dp = mesh.shape["seq"], mesh.shape["dp"]
-    across = min(4, n_seq // 4)
-    split = (n_seq // (2 * across), across, 2)
-
     def step(*args):
         rows, width = args[0].shape
         many = args[2].shape[0]
@@ -281,7 +276,7 @@
         hbm = pl.BlockSpec(memory_space=pltpu.HBM)
         on_chip = pl.BlockSpec(memory_space=pltpu.VMEM)
         results = pl.pallas_call(
-            functools.partial(kernel, n_seq, n_dp, split),
+            functools.partial(kernel, n_seq, n_dp),
             out_shape=[vmem(s, BF16) for s in out_shapes] + [vmem((width,), F32)],
             in_specs=[hbm] * 8,
             out_specs=[on_chip] * 7,

time: 28.8 us -> 28.9 us (level)
  no operation moved by 1% of the time
where the time goes in v5:
time: 28.9 us; the launch traced here: 28.8 us
  Pallas kernels  28.1 us (97%)
  between operations  0.64 us (2%)
    pallas_call x1, Pallas kernels, step(): pl.pallas_call(functools.partial(kernel, n_seq, n_dp), out_shape=[vmem(s,...  27.1 us
    pallas_call x1, Pallas kernels, step(): pl.pallas_call(write_back, out_shape=[jax.ShapeDtypeStruct(s, BF16) for s...  1 us

profile of v5, /device:TPU:1, one launch (start us, length us, event | category | flops | bytes accessed | tf_op | source)
XLA Modules:
  0.0 28.8 jit_solution(4501254167140197985)
XLA Ops:
  0.6 27.1 %shard_map.135 = (bf16[128,256]{1,0:T(8,128)(2,1)S(1)}, bf16[512,256]{1,0:T(8,128)(2,1)S(1)}, bf16[512,256]{1,0:T(8,128)(2,1)S(1)}, bf16[512,256]{1,0:T(8,128)(2...) custom-call(bf16[128,256]{1,0:T(8,128)(2,1)} %sq_h.1, bf16[128,256]{1,0:T(8,128)(2,1)} %og_h.1, ...), custom_call_target="tpu_custom_call" | custom-call | tf_op jit(solution)/shard_map/pallas_call | solution.py:278
  27.8 1.0 %shard_map.136 = (bf16[128,256]{1,0:T(8,128)(2,1)}, bf16[512,256]{1,0:T(8,128)(2,1)}, bf16[512,256]{1,0:T(8,128)(2,1)}, bf16[512,256]{1,0:T(8,128)(2,1)}, bf16[1...) custom-call(bf16[128,256]{1,0:T(8,128)(2,1)S(1)} %get-tuple-element.14.refs_0_, ...), custom_call_target="tpu_custom_call" | custom-call | tf_op jit(solution)/shard_map/pallas_call | solution.py:301

commit v6 on v5

--- a/solution.py
+++ b/solution.py
@@ -13,6 +13,7 @@
 NORM_EPS = 1e-05
 SCALE = HD ** (-0.5)
 MESH = pl.DeviceIdType.MESH
+HUB = 1
 F32 = jnp.float32
 BF16 = jnp.bfloat16
 
@@ -48,28 +49,27 @@
 
 
 def kernel(
-    n_seq, n_dp, sq_h, og_h, nk_h, ns_h, eq_h, sk_h, sv_h, gain_h,
+    n_seq, n_dp, n_add, sq_h, og_h, nk_h, ns_h, eq_h, sk_h, sv_h, gain_h,
     qg, kg, sg, eqg, skg, svg, gg,
     sq, og, nk, ns, eq, sk, sv, gain,
     next_q, next_g, dq_out, dq_in, enc, enc_w, enc_low, val, weights,
-    square_out, square_in, dot_out, dot_in, gain_out, gain_in,
+    square_out, square_in, square_sum, dot_out, dot_in, dot_sum, gain_out, gain_in,
     in_sem, halo_send, halo_recv, back_send, back_recv,
-    square_send, square_recv, dot_send, dot_recv, gain_send, gain_recv,
+    square_send, square_recv, square_send2, square_recv2, dot_send, dot_recv, dot_send2, dot_recv2, here, all_here, gain_send, gain_recv,
 ):
     seq, dp = lax.axis_index("seq"), lax.axis_index("dp")
     before = lax.rem(seq + n_seq - 1, n_seq)
     after = lax.rem(seq + 1, n_seq)
     width = n_dp * 2 * HD
 
-    def falling(me, n):
-        return [n - 1 - k - lax.div(me + k + 1, n) for k in range(n - 1)]
-
     def rising(me, n):
         above = [lax.div(me - k + n - 1, n) for k in range(n - 1)]
         return [(k + 1 - up, me - up) for k, up in enumerate(above)]
 
-    dp_peers = [((seq, peer), slot) for peer, slot in rising(dp, n_dp)]
+    dp_peers = [(seq, peer) for peer, _ in rising(dp, n_dp)]
     seq_peers = [((peer, dp), slot) for peer, slot in rising(seq, n_seq)]
+    adds = dp < n_add
+    is_hub = seq == HUB
 
     loads = {}
     for k, (name, src, dst) in enumerate([
@@ -80,9 +80,20 @@
         loads[name].start()
 
     barrier = pltpu.get_barrier_semaphore()
-    peers = [(seq, peer) for peer in falling(dp, n_dp)] + [(peer, dp) for peer in falling(seq, n_seq)]
-    for peer in peers:
-        pl.semaphore_signal(barrier, inc=1, device_id=peer, device_id_type=MESH)
+
+    def greet(peers):
+        for peer in peers:
+            pl.semaphore_signal(barrier, inc=1, device_id=peer, device_id_type=MESH)
+
+    greet([(before, dp), (after, dp)])
+
+    @pl.when(adds)
+    def _():
+        greet(dp_peers)
+
+    @pl.when(is_hub)
+    def _():
+        greet([peer for peer, _ in seq_peers])
 
     left = lax.broadcasted_iota(jnp.int32, (MEM, 2 * SPAN), 1) < SPAN
     tiles = 2 * MEM // 8
@@ -119,23 +130,45 @@
     def column(x):
         return jnp.sum(jnp.where(pick, x[None], 0.0), axis=2, keepdims=True).reshape(2 * MEM, 1)
 
+    def parts(out, into, send, recv, act):
+        for k in range(n_add):
+            @pl.when(dp != k)
+            def _():
+                act(pltpu.make_async_remote_copy(
+                    src_ref=out, dst_ref=into.at[dp - jnp.where(dp > k, 1, 0)], send_sem=send, recv_sem=recv,
+                    device_id=(seq, k), device_id_type=MESH))
+
+    def answers(total, send, recv, act):
+        for k in range(1, n_dp // n_add):
+            act(pltpu.make_async_remote_copy(
+                src_ref=total, dst_ref=total, send_sem=send, recv_sem=recv,
+                device_id=(seq, dp + k * n_add), device_id_type=MESH))
+
+    def begin(copy):
+        copy.start()
+
+    def left_here(copy):
+        copy.wait_send()
+
     def exchange(mine, out, into, send, recv):
         out[...] = mine
-        copies = [
-            pltpu.make_async_remote_copy(
-                src_ref=out, dst_ref=into.at[slot], send_sem=send, recv_sem=recv,
-                device_id=peer, device_id_type=MESH)
-            for peer, slot in dp_peers
-        ]
-        for copy in copies:
-            copy.start()
-
-    def gather(out, into, recv):
-        pltpu.make_async_copy(into, into, recv).wait()
-        return out[...] + jnp.sum(into[...], axis=0)
+        parts(out, into, send, recv, begin)
+
+    def gather(out, into, recv, total, total_send, total_recv):
+        @pl.when(adds)
+        def _():
+            pltpu.make_async_copy(into, into, recv).wait()
+            total[...] = out[...] + jnp.sum(into[...], axis=0)
+            answers(total, total_send, total_recv, begin)
+
+        @pl.when(jnp.logical_not(adds))
+        def _():
+            pltpu.make_async_copy(total, total, total_recv).wait()
+
+        return total[...]
 
     squares = packed(squares)
-    pl.semaphore_wait(barrier, len(peers))
+    pl.semaphore_wait(barrier, 2 + n_add - jnp.where(adds, 1, 0) + jnp.where(is_hub, 0, 1))
 
     halo = [
         pltpu.make_async_remote_copy(
@@ -147,6 +180,11 @@
         copy.start()
 
     exchange(squares, square_out, square_in, square_send, square_recv)
+
+    @pl.when(jnp.logical_not(is_hub))
+    def _():
+        pl.semaphore_signal(here, inc=1, device_id=(HUB, dp), device_id_type=MESH)
+
 
     loads["sq"].wait()
     loads["og"].wait()
@@ -172,6 +210,12 @@
     for c in range(2):
         rows = pl.ds(c * MEM, MEM)
         if c == 1:
+            @pl.when(is_hub)
+            def _():
+                pl.semaphore_wait(here, n_seq - 1)
+                for peer, _ in seq_peers:
+                    pl.semaphore_signal(all_here, inc=1, device_id=peer, device_id_type=MESH)
+
             for copy in halo:
                 copy.wait_recv()
         q, g = tokens(c)
@@ -185,7 +229,7 @@
         dots.append(fold(v * gains * enc[rows, :]))
 
     exchange(packed(dots), dot_out, dot_in, dot_send, dot_recv)
-    inverse = lax.rsqrt(gather(square_out, square_in, square_recv) * (1.0 / width) + NORM_EPS)
+    inverse = lax.rsqrt(gather(square_out, square_in, square_recv, square_sum, square_send2, square_recv2) * (1.0 / width) + NORM_EPS)
     packed_inverse = inverse
     inverse = column(inverse)
 
@@ -196,6 +240,10 @@
         own = own + jnp.sum(term.reshape(MEM // 8, 8, 2 * HD), axis=0)
     own = jnp.sum(own, axis=0, keepdims=True)
     gain_out[...] = jnp.concatenate([own[:, :HD], own[:, HD:]], axis=0)
+    @pl.when(jnp.logical_not(is_hub))
+    def _():
+        pl.semaphore_wait(all_here, 1)
+
     sums = [
         pltpu.make_async_remote_copy(
             src_ref=gain_out, dst_ref=gain_in.at[slot], send_sem=gain_send, recv_sem=gain_recv,
@@ -223,7 +271,7 @@
             back.start()
         kg[rows, :] = nn(d_s, q).astype(BF16)
 
-    grad_dot = gather(dot_out, dot_in, dot_recv)
+    grad_dot = gather(dot_out, dot_in, dot_recv, dot_sum, dot_send2, dot_recv2)
     slope = column(grad_dot * packed_inverse * packed_inverse * packed_inverse * (1.0 / width))
     for c in range(2):
         rows = pl.ds(c * MEM, MEM)
@@ -248,10 +296,17 @@
 
     for copy in halo + [back]:
         copy.wait_send()
-    for slots, sem in ((square_in, square_send), (dot_in, dot_send), (gain_in, gain_send)):
-        pltpu.make_async_copy(slots, slots, sem).wait()
-
-    total = gather(gain_out, gain_in, gain_recv)
+    parts(square_out, square_in, square_send, square_recv, left_here)
+    parts(dot_out, dot_in, dot_send, dot_recv, left_here)
+
+    @pl.when(adds)
+    def _():
+        answers(square_sum, square_send2, square_recv2, left_here)
+        answers(dot_sum, dot_send2, dot_recv2, left_here)
+
+    pltpu.make_async_copy(gain_in, gain_in, gain_send).wait()
+    pltpu.make_async_copy(gain_in, gain_in, gain_recv).wait()
+    total = gain_out[...] + jnp.sum(gain_in[...], axis=0)
     gg[...] = jnp.concatenate([total[0:1], total[1:2]], axis=1).reshape(2 * HD)
 
 
@@ -276,7 +331,7 @@
         hbm = pl.BlockSpec(memory_space=pltpu.HBM)
         on_chip = pl.BlockSpec(memory_space=pltpu.VMEM)
         results = pl.pallas_call(
-            functools.partial(kernel, n_seq, n_dp),
+            functools.partial(kernel, n_seq, n_dp, min(4, n_dp // 2)),
             out_shape=[vmem(s, BF16) for s in out_shapes] + [vmem((width,), F32)],
             in_specs=[hbm] * 8,
             out_specs=[on_chip] * 7,
@@ -288,11 +343,12 @@
             + [
                 vmem(large, F32), vmem((many, 2 * SPAN), F32), vmem((many, 2 * SPAN), BF16),
                 vmem(large, F32), vmem((many, 2 * SPAN), F32),
-                vmem((8, 128), F32), vmem((n_dp - 1, 8, 128), F32),
-                vmem((8, 128), F32), vmem((n_dp - 1, 8, 128), F32),
+                vmem((8, 128), F32), vmem((n_dp - 1, 8, 128), F32), vmem((8, 128), F32),
+                vmem((8, 128), F32), vmem((n_dp - 1, 8, 128), F32), vmem((8, 128), F32),
                 vmem((2, HD), F32), vmem((n_seq - 1, 2, HD), F32),
                 dma((8,)), dma((2,)), dma((2,)), dma, dma,
-                dma, dma, dma, dma, dma, dma,
+                dma, dma, dma, dma, dma, dma, dma, dma,
+                pltpu.SemaphoreType.REGULAR, pltpu.SemaphoreType.REGULAR, dma, dma,
             ],
             compiler_params=pltpu.CompilerParams(
                 collective_id=0, has_side_effects=True, vmem_limit_bytes=58 * 1024 * 1024

time: 28.9 us -> 27 us (0.934)
  Pallas kernels: 28.1 us -> 26.2 us
    pallas_call x1, Pallas kernels: 27.1 us -> 25.2 us  [step(): pl.pallas_call(functools.partial(kernel, n_seq, n_dp, min(4, n_dp // 2)),...]
where the time goes in v6:
time: 27 us; the launch traced here: 26.9 us
  Pallas kernels  26.2 us (97%)
  between operations  0.64 us (2%)
    pallas_call x1, Pallas kernels, step(): pl.pallas_call(functools.partial(kernel, n_seq, n_dp, min(4, n_dp // 2)),...  25.2 us
    pallas_call x1, Pallas kernels, step(): pl.pallas_call(write_back, out_shape=[jax.ShapeDtypeStruct(s, BF16) for s...  1 us

profile of v6, /device:TPU:1, one launch (start us, length us, event | category | flops | bytes accessed | tf_op | source)
XLA Modules:
  0.0 26.9 jit_solution(7702023189417815767)
XLA Ops:
  0.6 25.2 %shard_map.135 = (bf16[128,256]{1,0:T(8,128)(2,1)S(1)}, bf16[512,256]{1,0:T(8,128)(2,1)S(1)}, bf16[512,256]{1,0:T(8,128)(2,1)S(1)}, bf16[512,256]{1,0:T(8,128)(2...) custom-call(bf16[128,256]{1,0:T(8,128)(2,1)} %sq_h.1, bf16[128,256]{1,0:T(8,128)(2,1)} %og_h.1, ...), custom_call_target="tpu_custom_call" | custom-call | tf_op jit(solution)/shard_map/pallas_call | solution.py:333
  25.9 1.0 %shard_map.136 = (bf16[128,256]{1,0:T(8,128)(2,1)}, bf16[512,256]{1,0:T(8,128)(2,1)}, bf16[512,256]{1,0:T(8,128)(2,1)}, bf16[512,256]{1,0:T(8,128)(2,1)}, bf16[1...) custom-call(bf16[128,256]{1,0:T(8,128)(2,1)S(1)} %get-tuple-element.14.refs_0_, ...), custom_call_target="tpu_custom_call" | custom-call | tf_op jit(solution)/shard_map/pallas_call | solution.py:357

commit v7 on v6

--- a/solution.py
+++ b/solution.py
@@ -106,17 +106,18 @@
 
     loads["eq"].wait()
     loads["sk"].wait()
-    loads["sv"].wait()
-    loads["ns"].wait()
     squares = []
     for c in range(2):
         rows = pl.ds(c * MEM, MEM)
         keys = two_heads(sk[pl.ds(c * SPAN, SPAN), :])
-        values = two_heads(sv[pl.ds(c * SPAN, SPAN), :])
         e = jnp.exp(nt(eq[rows, :], keys) * SCALE)
         first, last = half_sums(e, left)
         w = e * jnp.where(left, 1.0 / first, 1.0 / last)
         low = w.astype(BF16)
+        if c == 0:
+            loads["sv"].wait()
+            loads["ns"].wait()
+        values = two_heads(sv[pl.ds(c * SPAN, SPAN), :])
         enc_w[rows, :] = w
         enc_low[rows, :] = low
         x = ns[rows, :].astype(F32) + nn(low, values)
@@ -169,6 +170,8 @@
 
     squares = packed(squares)
     pl.semaphore_wait(barrier, 2 + n_add - jnp.where(adds, 1, 0) + jnp.where(is_hub, 0, 1))
+
+    exchange(squares, square_out, square_in, square_send, square_recv)
 
     halo = [
         pltpu.make_async_remote_copy(
@@ -178,8 +181,6 @@
     ]
     for copy in halo:
         copy.start()
-
-    exchange(squares, square_out, square_in, square_send, square_recv)
 
     @pl.when(jnp.logical_not(is_hub))
     def _():

time: 27 us -> 26.9 us (level)
  no operation moved by 1% of the time
where the time goes in v7:
time: 26.9 us; the launch traced here: 26.8 us
  Pallas kernels  26.2 us (97%)
  between operations  0.64 us (2%)
    pallas_call x1, Pallas kernels, step(): pl.pallas_call(functools.partial(kernel, n_seq, n_dp, min(4, n_dp // 2)),...  25.2 us
    pallas_call x1, Pallas kernels, step(): pl.pallas_call(write_back, out_shape=[jax.ShapeDtypeStruct(s, BF16) for s...  1 us

profile of v7, /device:TPU:1, one launch (start us, length us, event | category | flops | bytes accessed | tf_op | source)
XLA Modules:
  0.0 26.8 jit_solution(8580397123130368141)
XLA Ops:
  0.6 25.2 %shard_map.135 = (bf16[128,256]{1,0:T(8,128)(2,1)S(1)}, bf16[512,256]{1,0:T(8,128)(2,1)S(1)}, bf16[512,256]{1,0:T(8,128)(2,1)S(1)}, bf16[512,256]{1,0:T(8,128)(2...) custom-call(bf16[128,256]{1,0:T(8,128)(2,1)} %sq_h.1, bf16[128,256]{1,0:T(8,128)(2,1)} %og_h.1, ...), custom_call_target="tpu_custom_call" | custom-call | tf_op jit(solution)/shard_map/pallas_call | solution.py:334
  25.8 1.0 %shard_map.136 = (bf16[128,256]{1,0:T(8,128)(2,1)}, bf16[512,256]{1,0:T(8,128)(2,1)}, bf16[512,256]{1,0:T(8,128)(2,1)}, bf16[512,256]{1,0:T(8,128)(2,1)}, bf16[1...) custom-call(bf16[128,256]{1,0:T(8,128)(2,1)S(1)} %get-tuple-element.14.refs_0_, ...), custom_call_target="tpu_custom_call" | custom-call | tf_op jit(solution)/shard_map/pallas_call | solution.py:358
